TPU v7x, 32 devices: a whole 2x2x4 slice. The times are simulated.
32 devices in a mesh: gx: 4 (over y, core), gy: 8 (over z, x).
Axes of the slice: x: 2, y: 2, z: 4, core: 2. Of those that a mesh axis runs over, the one named last changes fastest.
Arguments:
- slope_depth: float32 [1024, 4096], P('gx', 'gy'), may hold values from 0.2 to 2
- slope_momentum: float32 [2, 1024, 4096], P(None, 'gx', 'gy'), may hold values from -1.2 to 1.2
- bed_slope: float32 [2, 1024, 4096], P(None, 'gx', 'gy'), may hold values from -3 to 3
- friction: float32 [1024, 4096], P('gx', 'gy'), may hold values from 0.2 to 2
- slope_active: int32 [1024, 4096], P('gx', 'gy'), may hold values 0 or 1
- owners: int32 [4, 8, 256, 1], P('gx', 'gy'), may hold values from 0 to 31; in each aligned block of 256 rows (0 to 255, 256 to 511, ..., all dimensions but the last counted through in order) at most 16 rows name the same one
- offsets: int32 [4, 8, 256], P('gx', 'gy'), may hold values from 0 to 511
- lake_height: float32 [2048, 4096], P('gx', 'gy'), may hold values from -6 to 6
- lake_momentum: float32 [2, 2048, 4096], P(None, 'gx', 'gy'), may hold values from -16 to 16
- lake_diagonal: float32 [2048, 4096], P('gx', 'gy'), may hold values from 0.2 to 2
Outputs:
- slope_fields: float32 [3, 1024, 4096], P(None, 'gx', 'gy')
- new_height: float32 [2048, 4096], P('gx', 'gy')
- new_momentum: float32 [2, 2048, 4096], P(None, 'gx', 'gy')
Inputs may be any that keep to these rules, and one draw needn't show every extreme that they name: `owners`: among the 256 rows of one device, no owner is named by more than 16 rows, a bound that some block reaches.
All inputs are finite; a program needn't handle non-finite values. No bound on the sum of `slope_active` on one device may be relied on, other than what follows from the above.
Results may differ from a plain program's by a relative error of at most 0.0001.
Values sent between devices are 32-bit elements; how exact they have to be, the bound alone decides.
A program may use at most 128 MiB of HBM per device.

v0:
```python
import jax
import jax.numpy as jnp
from jax import lax
from jax.sharding import PartitionSpec as P

SECTIONS = 2
ITERS = 3


courant = 0.15
depth_floor = 0.25
dispersion = 0.5


def with_halo(shard, sides, width):
    for axis, dim in sides:
        peers, length = (lax.axis_size(axis), shard.shape[dim])
        up = [(i, (i + 1) % peers) for i in range(peers - 1)]
        down = [(j, i) for i, j in up]
        last = lax.slice_in_dim(shard, length - width, length, axis=dim)
        first = lax.slice_in_dim(shard, 0, width, axis=dim)
        before = lax.ppermute(last, axis, up)
        after = lax.ppermute(first, axis, down)
        shard = jnp.concatenate([before, shard, after], axis=dim)
    return shard


def advance(fields, padded, bed_slope, friction, active):
    height = padded[0]
    floored = jnp.maximum(height, depth_floor)
    along_speed = padded[1] / floored
    across_speed = padded[2] / floored
    pressure = 0.5 * height * height
    flux_along = jnp.stack([padded[1], padded[1] * along_speed + pressure, padded[2] * along_speed])
    flux_across = jnp.stack(
        [padded[2], padded[1] * across_speed, padded[2] * across_speed + pressure]
    )
    average = 0.25 * (
        padded[:, 2:, 1:-1] + padded[:, :-2, 1:-1] + padded[:, 1:-1, 2:] + padded[:, 1:-1, :-2]
    )
    update = average - 0.5 * courant * (flux_along[:, 2:, 1:-1] - flux_along[:, :-2, 1:-1])
    update = update - 0.5 * courant * (flux_across[:, 1:-1, 2:] - flux_across[:, 1:-1, :-2])
    forcing = jnp.stack(
        [
            jnp.zeros_like(fields[0]),
            fields[0] * bed_slope[0] - friction * fields[1],
            fields[0] * bed_slope[1] - friction * fields[2],
        ]
    )
    return (update + courant * forcing) * active[None]


def operate(vectors, lake_diagonal):
    padded = with_halo(vectors, (("gx", 1), ("gy", 2)), 1)
    beside = padded[:, 2:, 1:-1] + padded[:, :-2, 1:-1] + padded[:, 1:-1, 2:] + padded[:, 1:-1, :-2]
    return (1.0 + 4.0 * dispersion + lake_diagonal)[None] * vectors - dispersion * beside


def paired_sums(residual, applied):
    return lax.psum(
        (jnp.sum(residual * residual, axis=(1, 2)), jnp.sum(residual * applied, axis=(1, 2))),
        ("gx", "gy"),
    )


def per_device(
    slope_depth,
    slope_momentum,
    bed_slope,
    friction,
    slope_active,
    owners,
    offsets,
    lake_height,
    lake_momentum,
    lake_diagonal,
):
    active = slope_active.astype(jnp.float32)
    fields = jnp.concatenate([slope_depth[None], slope_momentum], axis=0)
    for section_index in range(SECTIONS):
        padded = with_halo(fields, (("gx", 1), ("gy", 2)), 1)
        fields = advance(fields, padded, bed_slope, friction, active)
    along_count = lax.axis_size("gx")
    across_count = lax.axis_size("gy")
    devices = along_count * across_count
    rows_here = fields.shape[1]
    columns = fields.shape[2]
    capacity = max(2, 2 * rows_here // devices)
    owner_list = owners.reshape(rows_here)
    offset_list = offsets.reshape(rows_here)
    matches = (owner_list[:, None] == jnp.arange(devices, dtype=jnp.int32)[None, :]).astype(
        jnp.int32
    )
    earlier = jnp.cumsum(matches, axis=0) - matches
    rank_in_owner = jnp.sum(earlier * matches, axis=1)
    slot_index = owner_list * capacity + rank_in_owner
    row_major = jnp.transpose(fields, (1, 0, 2))
    payload = jnp.zeros((devices * capacity, 3, columns), jnp.float32).at[slot_index].set(row_major)
    tags = (
        jnp.zeros((devices * capacity,), jnp.float32)
        .at[slot_index]
        .set((offset_list + 1).astype(jnp.float32))
    )
    payload = payload.reshape(devices, capacity, 3, columns)
    tags = tags.reshape(devices, capacity)
    received, got_tags = (
        lax.all_to_all(payload, ("gx", "gy"), split_axis=0, concat_axis=0, tiled=True),
        lax.all_to_all(tags, ("gx", "gy"), split_axis=0, concat_axis=0, tiled=True),
    )
    received = received.reshape(devices * capacity, 3, columns)
    got_tags = got_tags.reshape(devices * capacity).astype(jnp.int32)
    lake_rows = lake_height.shape[0]
    landing = jnp.where(got_tags > 0, got_tags - 1, lake_rows)
    placed = jnp.zeros((lake_rows + 1, 3, columns), jnp.float32).at[landing].add(received)
    inflow = jnp.transpose(placed[:lake_rows], (1, 0, 2))
    new_height = lake_height + inflow[0]
    right_side = lake_momentum + inflow[1:]
    solution = jnp.zeros_like(right_side)
    residual = right_side
    applied = operate(residual, lake_diagonal)
    norm_now, product = paired_sums(residual, applied)
    step_length = norm_now / product
    direction = residual
    along_image = applied
    for iteration in range(ITERS):
        solution = solution + step_length[:, None, None] * direction
        residual = residual - step_length[:, None, None] * along_image
        if iteration + 1 < ITERS:
            applied = operate(residual, lake_diagonal)
            norm_next, product = paired_sums(residual, applied)
            growth = norm_next / norm_now
            step_length = norm_next / (product - growth * norm_next / step_length)
            direction = residual + growth[:, None, None] * direction
            along_image = applied + growth[:, None, None] * along_image
            norm_now = norm_next
    return (fields, new_height, solution)


def solution(mesh):
    return jax.shard_map(
        per_device,
        mesh=mesh,
        in_specs=(
            P("gx", "gy"),
            P(None, "gx", "gy"),
            P(None, "gx", "gy"),
            P("gx", "gy"),
            P("gx", "gy"),
            P("gx", "gy", None, None),
            P("gx", "gy", None),
            P("gx", "gy"),
            P(None, "gx", "gy"),
            P("gx", "gy"),
        ),
        out_specs=(P(None, "gx", "gy"), P("gx", "gy"), P(None, "gx", "gy")),
        check_vma=False,
    )
```

profile of v0, /device:TPU:0, one launch (start us, length us, event | category | flops | bytes accessed | tf_op | source)
XLA Modules:
  0.0 523.7 jit_solution(5090294756021071245)
XLA Ops:
  1.5 2.4 collective-permute-start.1
  3.9 1.3 collective-permute-start
  6.7 1.9 fusion.50
  9.3 3.9 collective-permute-start.3
  13.2 1.3 collective-permute-start.2
  14.6 15.5 %collective-permute-done.3 = f32[3,258,1]{2,1,0:T(8,128)S(1)} collective-permute-done((f32[3,258,1]{2,1,0:T(8,128)S(1)}, f32[3,258,1]{2,1,0:T(8,128)S(1)}, u32[]{:S(2)}, u32[]{:S(2)}) %collective-permute-start.3) | collective-permute-done | bytes 3128 | tf_op jit(solution)/shard_map/ppermute | solution.py:22
  31.6 4.1 fusion.30
  35.8 3.7 collective-permute-start.5
  39.5 1.3 collective-permute-start.4
  40.8 1.4 scatter_custom_fusion
  42.9 9.4 %all-to-all-start = ((f32[32,1,16]{2,1,0:T(1,128)}), f32[32,1,16]{2,1,0:T(1,128)S(1)}, u32[]{:S(2)}, u32[]{:S(2)}) async-start(f32[32,1,16]{2,1,0:T(1,128)} %bitcast.19), calls=%async_computation | async-start | bytes 32768 | tf_op jit(solution)/shard_map/all_to_all | solution.py:108
  52.5 3.7 collective-permute-start.7
  56.2 1.8 collective-permute-start.6
  58.4 15.4 %collective-permute-done.7 = f32[3,258,1]{2,1,0:T(8,128)S(1)} collective-permute-done((f32[3,258,1]{2,1,0:T(8,128)S(1)}, f32[3,258,1]{2,1,0:T(8,128)S(1)}, u32[]{:S(2)}, u32[]{:S(2)}) %collective-permute-start.7) | collective-permute-done | bytes 3128 | tf_op jit(solution)/shard_map/ppermute | solution.py:22
  75.3 3.9 fusion.20
  79.2 1.1 copy-done.5
  80.4 1.1 copy.39
  81.4 2.5 broadcast_in_dim.16
  83.9 26.5 %scatter_fusion = f32[512,3,512]{2,1,0:T(4,128)} fusion(f32[512,3,512]{2,1,0:T(4,128)} %broadcast_in_dim.16, s32[256]{0:T(256)S(1)} %bitcast.108, f32[256,3,512]{2,1,0:T(4,128)S(1)} %copy.39), kind=kCustom, calls=%fused_computation.1 | custom fusion | bytes 4719616 | tf_op jit(solution)/shard_map/scatter | solution.py:98
  110.4 5.2 copy.40
  115.6 6.6 %all-to-all-start.1 = ((f32[32,16,3,512]{3,1,2,0:T(8,128)}), f32[32,16,3,512]{3,1,2,0:T(8,128)S(1)}, u32[]{:S(2)}, u32[]{:S(2)}) async-start(f32[32,16,3,512]{3,1,2,0:T(8,128)} %copy.40), calls=%async_computation.1 | async-start | bytes 6291456 | tf_op jit(solution)/shard_map/all_to_all | solution.py:107
  122.4 72.5 %all-to-all-done.1 = f32[32,16,3,512]{3,1,2,0:T(8,128)S(1)} async-done(((f32[32,16,3,512]{3,1,2,0:T(8,128)}), f32[32,16,3,512]{3,1,2,0:T(8,128)S(1)}, u32[]{:S(2)}, u32[]{:S(2)}) %all-to-all-start.1) | async-done | bytes 3145760 | tf_op jit(solution)/shard_map/all_to_all | solution.py:107
  195.2 4.1 copy.42
  199.3 2.5 broadcast_in_dim.13
  201.8 66.9 %scatter_fusion.1 = f32[513,3,512]{2,1,0:T(4,128)} fusion(f32[513,3,512]{2,1,0:T(4,128)} %broadcast_in_dim.13, s32[512]{0:T(512)S(1)} %bitcast.106, f32[512,3,512]{2,1,0:T(4,128)} %copy.42), kind=kCustom, calls=%fused_computation.2 | custom fusion | flops 786432 | bytes 9439232 | tf_op jit(solution)/shard_map/scatter-add | solution.py:114
  268.7 3.1 slice_bitcast_fusion
  271.8 2.3 slice_add_fusion
  274.1 1.3 collective-permute-start.9
  275.4 1.3 collective-permute-start.8
  276.7 1.7 collective-permute-done.8
  279.7 4.1 collective-permute-start.11
  283.8 1.3 collective-permute-start.10
  285.1 1.3 broadcast_add_fusion
  286.4 2.9 collective-permute-done.10
  289.3 1.1 copy.45
  291.5 16.1 %multiply_reduce_fusion.3 = (f32[2]{0:T(128)S(1)}, f32[2]{0:T(128)S(1)}, f32[2,512,512]{2,0,1:T(2,128)}) fusion(f32[2,512,512]{2,0,1:T(2,128)S(1)} %slice_add_fusion, f32[2,1,512]{2,0,1:T(2,128)S(1)} %collective-permute-done.8, f32[2,1,512]{2,0,1:T(2,128)S(1)} %collective-permute-done.9, f32[2,514,1]{2,0,1:T(2,128)} %copy.47, f32[2,514,1]{2,0,1:T(2,128)} %copy.45, ...), kind=kLoop, calls=%fused_computation.51 | loop fusion | flops 9437180 | bytes 5259312 | tf_op jit(solution)/shard_map/reduce_sum | solution.py:61
  307.6 41.6 %all-reduce.2 = (f32[2]{0:T(128)S(1)}, f32[2]{0:T(128)S(1)}) all-reduce(f32[2]{0:T(128)S(1)} %get-tuple-element.17, f32[2]{0:T(128)S(1)} %get-tuple-element.16), channel_id=1, replica_groups=mesh['gx'=4,'gy'=8] {'gx','gy'}, use_global_device_ids=true, to_apply=%region_7.8 | all-reduce | flops 4 | bytes 32 | tf_op jit(solution)/shard_map/psum | solution.py:60
  349.2 2.7 multiply_subtract_fusion.1
  352.0 1.3 collective-permute-start.13
  353.3 1.3 collective-permute-start.12
  354.6 4.3 collective-permute-done.12
  358.8 1.8 pad_maximum_fusion.55
  360.6 1.3 copy.48
  361.9 1.3 collective-permute-start.14
  363.2 1.3 copy.50
  364.4 4.5 collective-permute-start.15
  369.0 1.1 copy.49
  371.4 17.1 %multiply_reduce_fusion.1 = (f32[2]{0:T(128)S(1)}, f32[2]{0:T(128)S(1)}, f32[2,512,512]{2,0,1:T(2,128)}) fusion(f32[2,512,512]{2,0,1:T(2,128)} %copy-done, f32[2,1,512]{2,0,1:T(2,128)S(1)} %collective-permute-done.12, f32[2,1,512]{2,0,1:T(2,128)S(1)} %collective-permute-done.13, f32[2,514,1]{2,0,1:T(2,128)} %copy.51, f32[2,514,1]{2,0,1:T(2,128)} %copy.49, ...), kind=kLoop, calls=%fused_computation.48 | loop fusion | flops 9437180 | bytes 5259312 | tf_op jit(solution)/shard_map/reduce_sum | solution.py:61
  388.5 40.8 %all-reduce.1 = (f32[2]{0:T(128)S(1)}, f32[2]{0:T(128)S(1)}) all-reduce(f32[2]{0:T(128)S(1)} %get-tuple-element.15, f32[2]{0:T(128)S(1)} %get-tuple-element.14), channel_id=1, replica_groups=mesh['gx'=4,'gy'=8] {'gx','gy'}, use_global_device_ids=true, to_apply=%region_11.12 | all-reduce | flops 4 | bytes 32 | tf_op jit(solution)/shard_map/psum | solution.py:60
  429.3 4.4 multiply_subtract_fusion
  433.7 1.3 collective-permute-start.17
  435.0 1.3 collective-permute-start.16
  436.3 3.9 slice.320
  440.5 1.7 pad_maximum_fusion.52
  442.3 1.3 copy.52
  443.5 1.3 copy.54
  444.8 3.9 collective-permute-start.19
  448.7 1.5 collective-permute-start.18
  450.3 2.7 bitcast_add_fusion
  453.0 1.2 collective-permute-done.18
  456.3 17.4 %fusion.16 = (f32[2]{0:T(128)S(1)}, f32[2]{0:T(128)S(1)}) fusion(f32[2,512,512]{2,0,1:T(2,128)} %copy-done.1, f32[2,1,512]{2,0,1:T(2,128)S(1)} %collective-permute-done.16, f32[2,1,512]{2,0,1:T(2,128)S(1)} %collective-permute-done.17, f32[2,514,1]{2,0,1:T(2,128)} %copy.55, f32[2,514,1]{2,0,1:T(2,128)} %copy.53, f32[512,512]{1,0:T(8,128)S(1)} %broadcast_add_fusion), kind=kLoop, calls=%fused_computation.53 | loop fusion | flops 9437180 | bytes 3162160 | tf_op jit(solution)/shard_map/reduce_sum | solution.py:61
  473.7 43.9 %all-reduce = (f32[2]{0:T(128)S(1)}, f32[2]{0:T(128)S(1)}) all-reduce(f32[2]{0:T(128)S(1)} %get-tuple-element.13, f32[2]{0:T(128)S(1)} %get-tuple-element.12), channel_id=1, replica_groups=mesh['gx'=4,'gy'=8] {'gx','gy'}, use_global_device_ids=true, to_apply=%region_15.16 | all-reduce | flops 4 | bytes 32 | tf_op jit(solution)/shard_map/psum | solution.py:60
  517.6 4.2 multiply_add_fusion
  521.8 1.7 copy.56
  (78 shorter events, 13.8 us)
Async XLA Ops:
  0.6 6.0 %copy-start.2 = (f32[2,256,512]{2,1,0:T(8,128)S(1)}, f32[2,256,512]{2,1,0:T(8,128)}, u32[]{:S(2)}) copy-start(f32[2,256,512]{2,1,0:T(8,128)} %param.11) | copy-start | bytes 3145732
  1.5 7.2 %collective-permute-start.1 = (f32[3,1,512]{2,1,0:T(1,128)S(1)}, f32[3,1,512]{2,1,0:T(1,128)S(1)}, u32[]{:S(2)}, u32[]{:S(2)}) collective-permute-start(f32[3,1,512]{2,1,0:T(1,128)S(1)} %get-tuple-element.65), channel_id=1, source_target_pairs={{0,8},{8,16},{16,24},{1,9},{9,17},{17,25},{2,10},{10,18},{18,26},{... | collective-permute-start | bytes 18440 | tf_op jit(solution)/shard_map/ppermute | solution.py:22
  3.9 5.2 collective-permute-start
  6.7 2.0 copy-start.10
  6.7 2.4 copy-start.3
  8.6 5.9 %copy-start.9 = (s32[256,512]{1,0:T(8,128)S(1)}, s32[256,512]{1,0:T(8,128)}, u32[]{:S(2)}) copy-start(s32[256,512]{1,0:T(8,128)} %param.14) | copy-start | bytes 1572868
  9.3 20.8 %collective-permute-start.3 = (f32[3,258,1]{2,1,0:T(8,128)S(1)}, f32[3,258,1]{2,1,0:T(8,128)S(1)}, u32[]{:S(2)}, u32[]{:S(2)}) collective-permute-start(f32[3,258,1]{2,1,0:T(8,128)S(1)} %get-tuple-element.61), channel_id=1, source_target_pairs={{0,1},{1,2},{2,3},{3,4},{4,5},{5,6},{6,7},{8,9},{9,10},{10,11},{11... | collective-permute-start | bytes 9296 | tf_op jit(solution)/shard_map/ppermute | solution.py:22
  13.2 16.9 %collective-permute-start.2 = (f32[3,258,1]{2,1,0:T(8,128)S(1)}, f32[3,258,1]{2,1,0:T(8,128)S(1)}, u32[]{:S(2)}, u32[]{:S(2)}) collective-permute-start(f32[3,258,1]{2,1,0:T(8,128)S(1)} %get-tuple-element.62), channel_id=1, source_target_pairs={{1,0},{2,1},{3,2},{4,3},{5,4},{6,5},{7,6},{9,8},{10,9},{11,10},{12... | collective-permute-start | bytes 9296 | tf_op jit(solution)/shard_map/ppermute | solution.py:23
  31.6 9.2 %copy-start.11 = (s32[1,1,256]{2,1,0:T(1,128)S(1)}, s32[1,1,256]{2,1,0:T(1,128)}, u32[]{:S(2)}) copy-start(s32[1,1,256]{2,1,0:T(1,128)} %param.16) | copy-start | bytes 3076
  35.8 22.3 %copy-start.6 = (f32[2,256,512]{2,1,0:T(8,128)S(1)}, f32[2,256,512]{2,1,0:T(8,128)}, u32[]{:S(2)}) copy-start(f32[2,256,512]{2,1,0:T(8,128)} %param.12) | copy-start | bytes 3145732
  35.8 16.5 %collective-permute-start.5 = (f32[3,1,512]{2,1,0:T(1,128)S(1)}, f32[3,1,512]{2,1,0:T(1,128)S(1)}, u32[]{:S(2)}, u32[]{:S(2)}) collective-permute-start(f32[3,1,512]{2,1,0:T(1,128)S(1)} %get-tuple-element.63), channel_id=1, source_target_pairs={{0,8},{8,16},{16,24},{1,9},{9,17},{17,25},{2,10},{10,18},{18,26},{... | collective-permute-start | bytes 18440 | tf_op jit(solution)/shard_map/ppermute | solution.py:22
  39.5 12.8 %collective-permute-start.4 = (f32[3,1,512]{2,1,0:T(1,128)S(1)}, f32[3,1,512]{2,1,0:T(1,128)S(1)}, u32[]{:S(2)}, u32[]{:S(2)}) collective-permute-start(f32[3,1,512]{2,1,0:T(1,128)S(1)} %get-tuple-element.64), channel_id=1, source_target_pairs={{8,0},{16,8},{24,16},{9,1},{17,9},{25,17},{10,2},{18,10},{26,18},{... | collective-permute-start | bytes 18440 | tf_op jit(solution)/shard_map/ppermute | solution.py:23
  42.9 72.7 %all-to-all-start = ((f32[32,1,16]{2,1,0:T(1,128)}), f32[32,1,16]{2,1,0:T(1,128)S(1)}, u32[]{:S(2)}, u32[]{:S(2)}) async-start(f32[32,1,16]{2,1,0:T(1,128)} %bitcast.19), calls=%async_computation | async-start | bytes 32768 | tf_op jit(solution)/shard_map/all_to_all | solution.py:108
  52.3 5.8 %copy-start.8 = (f32[256,512]{1,0:T(8,128)S(1)}, f32[256,512]{1,0:T(8,128)}, u32[]{:S(2)}) copy-start(f32[256,512]{1,0:T(8,128)} %param.13) | copy-start | bytes 1572868
  52.5 21.3 %collective-permute-start.7 = (f32[3,258,1]{2,1,0:T(8,128)S(1)}, f32[3,258,1]{2,1,0:T(8,128)S(1)}, u32[]{:S(2)}, u32[]{:S(2)}) collective-permute-start(f32[3,258,1]{2,1,0:T(8,128)S(1)} %get-tuple-element.59), channel_id=1, source_target_pairs={{0,1},{1,2},{2,3},{3,4},{4,5},{5,6},{6,7},{8,9},{9,10},{10,11},{11... | collective-permute-start | bytes 9296 | tf_op jit(solution)/shard_map/ppermute | solution.py:22
  56.2 17.6 %collective-permute-start.6 = (f32[3,258,1]{2,1,0:T(8,128)S(1)}, f32[3,258,1]{2,1,0:T(8,128)S(1)}, u32[]{:S(2)}, u32[]{:S(2)}) collective-permute-start(f32[3,258,1]{2,1,0:T(8,128)S(1)} %get-tuple-element.60), channel_id=1, source_target_pairs={{1,0},{2,1},{3,2},{4,3},{5,4},{6,5},{7,6},{9,8},{10,9},{11,10},{12... | collective-permute-start | bytes 9296 | tf_op jit(solution)/shard_map/ppermute | solution.py:23
  79.2 1.1 copy-start.5
  115.6 79.3 %all-to-all-start.1 = ((f32[32,16,3,512]{3,1,2,0:T(8,128)}), f32[32,16,3,512]{3,1,2,0:T(8,128)S(1)}, u32[]{:S(2)}, u32[]{:S(2)}) async-start(f32[32,16,3,512]{3,1,2,0:T(8,128)} %copy.40), calls=%async_computation.1 | async-start | bytes 6291456 | tf_op jit(solution)/shard_map/all_to_all | solution.py:107
  268.7 3.1 copy-start.7
  271.8 2.3 copy-start.4
  274.1 2.6 collective-permute-start.9
  275.4 3.1 collective-permute-start.8
  279.7 10.7 %collective-permute-start.11 = (f32[2,514,1]{1,0,2:T(2,128)S(1)}, f32[2,514,1]{1,0,2:T(2,128)S(1)}, u32[]{:S(2)}, u32[]{:S(2)}) collective-permute-start(f32[2,514,1]{1,0,2:T(2,128)S(1)} %copy.46), channel_id=1, source_target_pairs={{0,1},{1,2},{2,3},{3,4},{4,5},{5,6},{6,7},{8,9},{9,10},{10,11},{11... | collective-permute-start | bytes 12344 | tf_op jit(solution)/shard_map/ppermute | solution.py:22
  283.8 5.5 %collective-permute-start.10 = (f32[2,514,1]{1,0,2:T(2,128)S(1)}, f32[2,514,1]{1,0,2:T(2,128)S(1)}, u32[]{:S(2)}, u32[]{:S(2)}) collective-permute-start(f32[2,514,1]{1,0,2:T(2,128)S(1)} %copy.44), channel_id=1, source_target_pairs={{1,0},{2,1},{3,2},{4,3},{5,4},{6,5},{7,6},{9,8},{10,9},{11,10},{12... | collective-permute-start | bytes 12344 | tf_op jit(solution)/shard_map/ppermute | solution.py:23
  352.0 6.9 %copy-start = (f32[2,512,512]{2,0,1:T(2,128)}, f32[2,512,512]{2,0,1:T(2,128)S(1)}, u32[]{:S(2)}) copy-start(f32[2,512,512]{2,0,1:T(2,128)S(1)} %multiply_subtract_fusion.1) | copy-start | bytes 6291460
  352.0 2.6 collective-permute-start.13
  353.3 5.6 %collective-permute-start.12 = (f32[2,1,512]{2,0,1:T(2,128)S(1)}, f32[2,1,512]{2,0,1:T(2,128)S(1)}, u32[]{:S(2)}, u32[]{:S(2)}) collective-permute-start(f32[2,1,512]{2,0,1:T(2,128)S(1)} %get-tuple-element.44), channel_id=1, source_target_pairs={{8,0},{16,8},{24,16},{9,1},{17,9},{25,17},{10,2},{18,10},{26,18},{... | collective-permute-start | bytes 12296 | tf_op jit(solution)/shard_map/ppermute | solution.py:23
  361.9 7.1 %collective-permute-start.14 = (f32[2,514,1]{1,0,2:T(2,128)S(1)}, f32[2,514,1]{1,0,2:T(2,128)S(1)}, u32[]{:S(2)}, u32[]{:S(2)}) collective-permute-start(f32[2,514,1]{1,0,2:T(2,128)S(1)} %copy.48), channel_id=1, source_target_pairs={{1,0},{2,1},{3,2},{4,3},{5,4},{6,5},{7,6},{9,8},{10,9},{11,10},{12... | collective-permute-start | bytes 12344 | tf_op jit(solution)/shard_map/ppermute | solution.py:23
  364.4 5.9 %collective-permute-start.15 = (f32[2,514,1]{1,0,2:T(2,128)S(1)}, f32[2,514,1]{1,0,2:T(2,128)S(1)}, u32[]{:S(2)}, u32[]{:S(2)}) collective-permute-start(f32[2,514,1]{1,0,2:T(2,128)S(1)} %copy.50), channel_id=1, source_target_pairs={{0,1},{1,2},{2,3},{3,4},{4,5},{5,6},{6,7},{8,9},{9,10},{10,11},{11... | collective-permute-start | bytes 12344 | tf_op jit(solution)/shard_map/ppermute | solution.py:22
  433.7 8.6 %copy-start.1 = (f32[2,512,512]{2,0,1:T(2,128)}, f32[2,512,512]{2,0,1:T(2,128)S(1)}, u32[]{:S(2)}) copy-start(f32[2,512,512]{2,0,1:T(2,128)S(1)} %multiply_subtract_fusion) | copy-start | bytes 6291460
  433.7 6.5 %collective-permute-start.17 = (f32[2,1,512]{2,0,1:T(2,128)S(1)}, f32[2,1,512]{2,0,1:T(2,128)S(1)}, u32[]{:S(2)}, u32[]{:S(2)}) collective-permute-start(f32[2,1,512]{2,0,1:T(2,128)S(1)} %get-tuple-element.41), channel_id=1, source_target_pairs={{0,8},{8,16},{16,24},{1,9},{9,17},{17,25},{2,10},{10,18},{18,26},{... | collective-permute-start | bytes 12296 | tf_op jit(solution)/shard_map/ppermute | solution.py:22
  435.0 5.6 %collective-permute-start.16 = (f32[2,1,512]{2,0,1:T(2,128)S(1)}, f32[2,1,512]{2,0,1:T(2,128)S(1)}, u32[]{:S(2)}, u32[]{:S(2)}) collective-permute-start(f32[2,1,512]{2,0,1:T(2,128)S(1)} %get-tuple-element.42), channel_id=1, source_target_pairs={{8,0},{16,8},{24,16},{9,1},{17,9},{25,17},{10,2},{18,10},{26,18},{... | collective-permute-start | bytes 12296 | tf_op jit(solution)/shard_map/ppermute | solution.py:23
  444.8 10.5 %collective-permute-start.19 = (f32[2,514,1]{1,0,2:T(2,128)S(1)}, f32[2,514,1]{1,0,2:T(2,128)S(1)}, u32[]{:S(2)}, u32[]{:S(2)}) collective-permute-start(f32[2,514,1]{1,0,2:T(2,128)S(1)} %copy.54), channel_id=1, source_target_pairs={{0,1},{1,2},{2,3},{3,4},{4,5},{5,6},{6,7},{8,9},{9,10},{10,11},{11... | collective-permute-start | bytes 12344 | tf_op jit(solution)/shard_map/ppermute | solution.py:22
  448.7 5.5 %collective-permute-start.18 = (f32[2,514,1]{1,0,2:T(2,128)S(1)}, f32[2,514,1]{1,0,2:T(2,128)S(1)}, u32[]{:S(2)}, u32[]{:S(2)}) collective-permute-start(f32[2,514,1]{1,0,2:T(2,128)S(1)} %copy.52), channel_id=1, source_target_pairs={{1,0},{2,1},{3,2},{4,3},{5,4},{6,5},{7,6},{9,8},{10,9},{11,10},{12... | collective-permute-start | bytes 12344 | tf_op jit(solution)/shard_map/ppermute | solution.py:23
where the time goes:
time: 531 us; the launch traced here: 524 us
  other arithmetic  155 us (29%)
  blocking collectives  126 us (24%)
  waiting for transfers between devices  114 us (21%)
  local copies, waits for them, and re-layouts  66.3 us (12%)
  starting transfers between devices  59.8 us (11%)
    psum x3, blocking collectives, paired_sums(): lax.psum((jnp.sum(residual * residual, axis=(1, 2)), jnp.sum(residual * a...  126 us
    all_to_all x1, waiting for transfers between devices, per_device(): lax.all_to_all(payload, ('gx', 'gy'), split_axis=0, concat_axis=0, tiled=...  72.5 us
    scatter-add x1, other arithmetic, per_device(): jnp.zeros((lake_rows + 1, 3, columns), jnp.float32).at[landing]  66.9 us
    reduce_sum x3, other arithmetic, paired_sums(): jnp.sum(residual * applied, axis=(1, 2))  50.6 us
    ppermute x10, waiting for transfers between devices, with_halo(): before = lax.ppermute(last, axis, up)  31.1 us
    ppermute x10, starting transfers between devices, with_halo(): before = lax.ppermute(last, axis, up)  30.1 us
    scatter x1, local copies, waits for them, and re-layouts, per_device(): jnp.zeros((devices * capacity, 3, columns), jnp.float32).at[slot_index]  26.5 us
    ppermute x10, starting transfers between devices, with_halo(): after = lax.ppermute(first, axis, down)  13.7 us
  transfers between devices with their start and end apart: 22, of which 10 were waited for; matrix products, arithmetic and copies ran while one was open for 11% of the time, Pallas kernels for 0%

commit v1 on v0

v1 whole, which is shorter than its diff:
```python
import functools

import jax
import jax.numpy as jnp
from jax import lax
from jax.experimental import pallas as pl
from jax.experimental.pallas import tpu as pltpu
from jax.sharding import PartitionSpec as P

SECTIONS = 2
courant = 0.15
depth_floor = 0.25
dispersion = 0.5
SHIFT = 4.1
PAD = 8
MESH = pl.DeviceIdType.MESH


def along_terms(h, m, n, sign):
    inv = 1.0 / jnp.maximum(h, depth_floor)
    u = m * inv
    k = sign * 0.5 * courant
    return (0.25 * h + k * m, 0.25 * m + k * (m * u + 0.5 * h * h), 0.25 * n + k * (n * u))


def across_terms(h, m, n, sign):
    inv = 1.0 / jnp.maximum(h, depth_floor)
    v = n * inv
    k = sign * 0.5 * courant
    return (0.25 * h + k * n, 0.25 * m + k * (m * v), 0.25 * n + k * (n * v + 0.5 * h * h))


def split3(x):
    hi = x.astype(jnp.bfloat16)
    rest = x - hi.astype(jnp.float32)
    mid = rest.astype(jnp.bfloat16)
    low = (rest - mid.astype(jnp.float32)).astype(jnp.bfloat16)
    return hi, mid, low


def column(x, lane):
    return jnp.transpose(x)[lane : lane + 1, :]


def as_column(row):
    return jnp.transpose(jnp.broadcast_to(row, (128, row.shape[1])))


def kernel(
    n0,
    n1,
    cap,
    depth_ref,
    mom_ref,
    bed_ref,
    fric_ref,
    act_ref,
    own_row_ref,
    own_col_ref,
    off_ref,
    lh_hbm,
    lm_hbm,
    ld_hbm,
    slope_out,
    height_out,
    lake_out,
    fields,
    parts,
    send,
    recv,
    tag_send,
    tag_recv,
    hot,
    rparts,
    vec,
    lh,
    ld,
    srow_s,
    srow_r,
    scol_s,
    scol_r,
    lrow_s,
    lrow_r,
    lcol_s,
    lcol_r,
    sum_s,
    sum_r,
    tag_ss,
    tag_rs,
    blk_ss,
    blk_rs,
    sl_ss,
    sl_rs,
    lk_ss,
    lk_rs,
    sum_ss,
    sum_rs,
    loc,
):
    n = n0 * n1
    gx = lax.axis_index("gx")
    gy = lax.axis_index("gy")
    me = gx * n1 + gy
    rows, cols = depth_ref.shape
    lrows = lh.shape[0]
    slots = n * cap
    f32 = jnp.float32

    def peer(k):
        return lax.rem(me + k, n)

    def coords(t):
        return (lax.div(t, n1), lax.rem(t, n1))

    load_m = [
        pltpu.make_async_copy(lm_hbm.at[c], vec.at[0, c, pl.ds(PAD, lrows), :], loc.at[c])
        for c in range(2)
    ]
    load_h = pltpu.make_async_copy(lh_hbm, lh, loc.at[2])
    load_d = pltpu.make_async_copy(ld_hbm, ld, loc.at[3])
    for c in load_m + [load_h, load_d]:
        c.start()

    barrier = pltpu.get_barrier_semaphore()

    def greet(k, carry):
        pl.semaphore_signal(barrier, inc=1, device_id=coords(peer(k)), device_id_type=MESH)
        return carry

    lax.fori_loop(1, n, greet, 0)

    own_row = own_row_ref[...]
    before = lax.broadcasted_iota(jnp.int32, (rows, rows), 0) < lax.broadcasted_iota(
        jnp.int32, (rows, rows), 1
    )
    rank = jnp.sum(
        jnp.where((own_col_ref[...] == own_row) & before, 1.0, 0.0), axis=0, keepdims=True
    )
    slot = own_row * cap + rank.astype(jnp.int32)
    off = (off_ref[...] + 1).astype(f32)
    SC = 128

    def chosen(j):
        return (lax.broadcasted_iota(jnp.int32, (SC, rows), 0) + j * SC) == slot

    def tags(j, carry):
        col = jnp.sum(jnp.where(chosen(j), off, 0.0), axis=1, keepdims=True)
        tag_send[pl.ds(pl.multiple_of(j * SC, SC), SC), :] = jnp.broadcast_to(col, (SC, 128))
        return carry

    lax.fori_loop(0, slots // SC, tags, 0)

    for c in range(3):
        for e in range(SECTIONS):
            fields[e, c, 0:PAD, :] = jnp.zeros((PAD, cols), f32)
            fields[e, c, PAD + rows : PAD + rows + PAD, :] = jnp.zeros((PAD, cols), f32)
    for c in range(2):
        for e in range(3):
            vec[e, c, 0:PAD, :] = jnp.zeros((PAD, cols), f32)
            vec[e, c, PAD + lrows : PAD + lrows + PAD, :] = jnp.zeros((PAD, cols), f32)
    fields[0, 0, PAD : PAD + rows, :] = depth_ref[...]
    fields[0, 1, PAD : PAD + rows, :] = mom_ref[0]
    fields[0, 2, PAD : PAD + rows, :] = mom_ref[1]

    pl.semaphore_wait(barrier, n - 1)

    def at(t):
        return pl.ds(pl.multiple_of(t * cap, cap), cap)

    def tag_copy(t, s):
        return pltpu.make_async_remote_copy(
            src_ref=tag_send.at[at(t), :],
            dst_ref=tag_recv.at[at(s), :],
            send_sem=tag_ss.at[t],
            recv_sem=tag_rs.at[s],
            device_id=coords(t),
            device_id_type=MESH,
        )

    def blk_copy(t, s):
        return pltpu.make_async_remote_copy(
            src_ref=send.at[at(t), :],
            dst_ref=recv.at[at(s), :],
            send_sem=blk_ss.at[t],
            recv_sem=blk_rs.at[s],
            device_id=coords(t),
            device_id_type=MESH,
        )

    neighbours = (
        (lax.rem(gx + 1, n0), gy),
        (lax.rem(gx + n0 - 1, n0), gy),
        (gx, lax.rem(gy + 1, n1)),
        (gx, lax.rem(gy + n1 - 1, n1)),
    )
    there = (gx > 0, gx < n0 - 1, gy > 0, gy < n1 - 1)

    def halo_copies(e, row_s, row_r, col_s, col_r, ss, rs):
        out = []
        for d in range(4):
            s, r = (row_s, row_r) if d < 2 else (col_s, col_r)
            out.append(
                pltpu.make_async_remote_copy(
                    src_ref=s.at[e, d % 2],
                    dst_ref=r.at[e, d % 2],
                    send_sem=ss.at[e, d],
                    recv_sem=rs.at[e, d],
                    device_id=neighbours[d],
                    device_id_type=MESH,
                )
            )
        return out

    pending = []
    RB = 64
    lane = lax.broadcasted_iota(jnp.int32, (RB, cols), 1)
    first_lane = lane == 0
    last_lane = lane == cols - 1

    def from_left(x):
        return jnp.where(first_lane, 0.0, pltpu.roll(x, 1, 1))

    def from_right(x):
        return jnp.where(last_lane, 0.0, pltpu.roll(x, cols - 1, 1))

    for e in range(SECTIONS):
        lo = [fields[e, c, PAD : PAD + 8, :] for c in range(3)]
        hi = [fields[e, c, PAD + rows - 8 : PAD + rows, :] for c in range(3)]
        for c, x in enumerate(along_terms(*hi, 1.0)):
            srow_s[e, 0, c : c + 1, :] = x[7:8, :]
        for c, x in enumerate(along_terms(*lo, -1.0)):
            srow_s[e, 1, c : c + 1, :] = x[0:1, :]
        right = [fields[e, c, PAD : PAD + rows, cols - 128 : cols] for c in range(3)]
        for c, x in enumerate(across_terms(*right, 1.0)):
            scol_s[e, 0, c : c + 1, :] = column(x, 127)
        left = [fields[e, c, PAD : PAD + rows, 0:128] for c in range(3)]
        for c, x in enumerate(across_terms(*left, -1.0)):
            scol_s[e, 1, c : c + 1, :] = column(x, 0)
        copies = halo_copies(e, srow_s, srow_r, scol_s, scol_r, sl_ss, sl_rs)
        for c in copies:
            c.start()
        pending += copies
        if e == 0:

            def send_tags(k, carry):
                tag_copy(peer(k), me).start()
                return carry

            lax.fori_loop(1, n, send_tags, 0)

        def section(i, carry):
            base = pl.multiple_of(i * RB, RB)
            x = [fields[e, c, pl.ds(base, RB + 2 * PAD), :] for c in range(3)]
            mid = [v[PAD : PAD + RB, :] for v in x]
            below = along_terms(*[v[PAD - 1 : PAD - 1 + RB, :] for v in x], 1.0)
            above = along_terms(*[v[PAD + 1 : PAD + 1 + RB, :] for v in x], -1.0)
            left = across_terms(*mid, 1.0)
            right = across_terms(*mid, -1.0)
            here = pl.ds(base, RB)
            active = act_ref[here, :].astype(f32)
            fric = fric_ref[here, :]
            for c in range(3):
                total = below[c] + above[c] + from_left(left[c]) + from_right(right[c])
                if c > 0:
                    total = total + courant * (mid[0] * bed_ref[c - 1, here, :] - fric * mid[c])
                fields[e + 1, c, pl.ds(pl.multiple_of(base + PAD, PAD), RB), :] = total * active
            return carry

        lax.fori_loop(0, rows // RB, section, 0)
        for c in copies:
            c.wait_recv()
        sub = lax.broadcasted_iota(jnp.int32, (8, cols), 0)
        tile_lane = lax.broadcasted_iota(jnp.int32, (rows, 128), 1)
        for d, (r0, at_row) in enumerate(((0, 0), (rows - 8, 7))):
            act = act_ref[r0 : r0 + 8, :].astype(f32)
            for c in range(3):
                add = jnp.where(
                    (sub == at_row) & there[d], act * srow_r[e, d, c : c + 1, :], 0.0
                )
                fields[e + 1, c, PAD + r0 : PAD + r0 + 8, :] += add
        for d, (c0, at_lane) in enumerate(((0, 0), (cols - 128, 127))):
            act = act_ref[:, c0 : c0 + 128].astype(f32)
            for c in range(3):
                add = jnp.where(
                    (tile_lane == at_lane) & there[2 + d],
                    act * as_column(scol_r[e, d, c : c + 1, :]),
                    0.0,
                )
                fields[e + 1, c, PAD : PAD + rows, c0 : c0 + 128] += add

    slope_store = pltpu.make_async_copy(
        fields.at[SECTIONS, :, pl.ds(PAD, rows), :], slope_out, loc.at[4]
    )
    slope_store.start()

    for c in range(3):
        pieces = split3(fields[SECTIONS, c, PAD : PAD + rows, :])
        for p in range(3):
            parts[p, :, c * cols : (c + 1) * cols] = pieces[p]

    def pack(j, carry):
        pick = jnp.where(chosen(j), 1.0, 0.0).astype(jnp.bfloat16)
        dst = pl.ds(pl.multiple_of(j * SC, SC), SC)
        for c in range(3):
            w = slice(c * cols, (c + 1) * cols)
            total = jnp.dot(pick, parts[2, :, w], preferred_element_type=f32)
            total += jnp.dot(pick, parts[1, :, w], preferred_element_type=f32)
            total += jnp.dot(pick, parts[0, :, w], preferred_element_type=f32)
            send[dst, w] = total
        return carry

    lax.fori_loop(0, slots // SC, pack, 0)

    def send_blocks(k, carry):
        blk_copy(peer(k), me).start()
        return carry

    lax.fori_loop(1, n, send_blocks, 0)
    own_tags = pltpu.make_async_copy(tag_send.at[at(me), :], tag_recv.at[at(me), :], loc.at[5])
    own_blk = pltpu.make_async_copy(send.at[at(me), :], recv.at[at(me), :], loc.at[6])
    own_tags.start()
    own_blk.start()

    def got_tags(k, carry):
        tag_copy(peer(k), peer(k)).wait_recv()
        return carry

    lax.fori_loop(1, n, got_tags, 0)
    own_tags.wait()
    tag_row = jnp.transpose(tag_recv[...])[0:1, :]

    def land(i, carry):
        want = (lax.broadcasted_iota(jnp.int32, (SC, slots), 0) + (i * SC + 1)).astype(f32)
        hot[pl.ds(pl.multiple_of(i * SC, SC), SC), :] = jnp.where(want == tag_row, 1.0, 0.0).astype(
            jnp.bfloat16
        )
        return carry

    lax.fori_loop(0, lrows // SC, land, 0)
    for c in load_m + [load_h, load_d]:
        c.wait()

    def got_blocks(k, carry):
        blk_copy(peer(k), peer(k)).wait_recv()
        return carry

    lax.fori_loop(1, n, got_blocks, 0)
    own_blk.wait()

    for c in range(3):

        def cut(j, carry):
            here = pl.ds(pl.multiple_of(j * SC, SC), SC)
            for p, piece in enumerate(split3(recv[here, c * cols : (c + 1) * cols])):
                rparts[p, here, :] = piece
            return carry

        lax.fori_loop(0, slots // SC, cut, 0)

        def inflow(i, carry):
            here = pl.ds(pl.multiple_of(i * SC, SC), SC)
            pick = hot[here, :]
            total = jnp.dot(pick, rparts[2], preferred_element_type=f32)
            total += jnp.dot(pick, rparts[1], preferred_element_type=f32)
            total += jnp.dot(pick, rparts[0], preferred_element_type=f32)
            if c == 0:
                lh[here, :] += total
            else:
                vec[0, c - 1, pl.ds(pl.multiple_of(i * SC + PAD, PAD), SC), :] += total
            return carry

        lax.fori_loop(0, lrows // SC, inflow, 0)
        if c == 0:
            height_store = pltpu.make_async_copy(lh, height_out, loc.at[2])
            height_store.start()

    spot = lax.broadcasted_iota(jnp.int32, (1, 128), 1)
    mine = jnp.zeros((1, 128), f32)
    for e in range(3):
        for c in range(2):
            lrow_s[e, 0, c : c + 1, :] = vec[e, c, PAD + lrows - 8 : PAD + lrows, :][7:8, :]
            lrow_s[e, 1, c : c + 1, :] = vec[e, c, PAD : PAD + 8, :][0:1, :]
            lcol_s[e, 0, c : c + 1, :] = column(
                vec[e, c, PAD : PAD + lrows, cols - 128 : cols], 127
            )
            lcol_s[e, 1, c : c + 1, :] = column(vec[e, c, PAD : PAD + lrows, 0:128], 0)
        copies = halo_copies(e, lrow_s, lrow_r, lcol_s, lcol_r, lk_ss, lk_rs)
        for c in copies:
            c.start()
        pending += copies

        def stencil(i, carry):
            base = pl.multiple_of(i * RB, RB)
            here = pl.ds(base, RB)
            diag = (1.0 + 4.0 * dispersion - SHIFT) + ld[here, :]
            result = []
            for c in range(2):
                x = vec[e, c, pl.ds(base, RB + 2 * PAD), :]
                mid = x[PAD : PAD + RB, :]
                beside = x[PAD - 1 : PAD - 1 + RB, :] + x[PAD + 1 : PAD + 1 + RB, :]
                beside = beside + from_left(mid) + from_right(mid)
                image = diag * mid - dispersion * beside
                if e < 2:
                    vec[e + 1, c, pl.ds(pl.multiple_of(base + PAD, PAD), RB), :] = image
                for q, term in enumerate((mid * mid, mid * image)):
                    result.append(
                        carry[2 * c + q] + jnp.sum(term.reshape(RB // 8, 8, cols), axis=0)
                    )
            return tuple(result)

        sums = lax.fori_loop(
            0, lrows // RB, stencil, tuple(jnp.zeros((8, cols), f32) for _ in range(4))
        )
        for c in copies:
            c.wait_recv()
        for c in range(2):
            halo_row = [
                jnp.where(there[d], lrow_r[e, d, c : c + 1, :], 0.0) for d in range(2)
            ]
            halo_col = [
                jnp.where(there[2 + d], lcol_r[e, d, c : c + 1, :], 0.0) for d in range(2)
            ]
            edge_r = lrow_s[e, 1, c : c + 1, :] * halo_row[0] + lrow_s[e, 0, c : c + 1, :] * halo_row[1]
            edge_c = lcol_s[e, 1, c : c + 1, :] * halo_col[0] + lcol_s[e, 0, c : c + 1, :] * halo_col[1]
            even = jnp.sum(sums[2 * c], axis=0, keepdims=True)
            odd = jnp.sum(sums[2 * c + 1], axis=0, keepdims=True) - dispersion * edge_r
            even = jnp.sum(even, axis=1, keepdims=True)
            odd = jnp.sum(odd, axis=1, keepdims=True) - dispersion * jnp.sum(
                edge_c, axis=1, keepdims=True
            )
            mine = jnp.where(spot == 6 * c + 2 * e, even, mine)
            mine = jnp.where(spot == 6 * c + 2 * e + 1, odd, mine)
            if e < 2:
                sub = lax.broadcasted_iota(jnp.int32, (8, cols), 0)
                for d, (r0, at_row) in enumerate(((0, 0), (lrows - 8, 7))):
                    vec[e + 1, c, PAD + r0 : PAD + r0 + 8, :] -= jnp.where(
                        sub == at_row, dispersion * halo_row[d], 0.0
                    )
                tile_lane = lax.broadcasted_iota(jnp.int32, (lrows, 128), 1)
                for d, (c0, at_lane) in enumerate(((0, 0), (cols - 128, 127))):
                    vec[e + 1, c, PAD : PAD + lrows, c0 : c0 + 128] -= jnp.where(
                        tile_lane == at_lane, dispersion * as_column(halo_col[d]), 0.0
                    )

    sum_s[...] = mine

    def sum_copy(t, s):
        return pltpu.make_async_remote_copy(
            src_ref=sum_s,
            dst_ref=sum_r.at[s],
            send_sem=sum_ss.at[t],
            recv_sem=sum_rs.at[s],
            device_id=coords(t),
            device_id_type=MESH,
        )

    def send_sums(k, carry):
        sum_copy(peer(k), me).start()
        return carry

    lax.fori_loop(1, n, send_sums, 0)

    for c in pending:
        c.wait_send()

    def sent(k, carry):
        tag_copy(peer(k), me).wait_send()
        blk_copy(peer(k), me).wait_send()
        return carry

    lax.fori_loop(1, n, sent, 0)

    def got_sums(k, total):
        s = peer(k)
        sum_copy(s, s).wait_recv()
        return total

    lax.fori_loop(1, n, got_sums, 0)
    sum_r[me] = mine
    total = jnp.sum(sum_r[...], axis=0)

    stores = []
    for c in range(2):
        nu = [
            jnp.sum(jnp.where(spot == 6 * c + k, total, 0.0), axis=1, keepdims=True)
            for k in range(6)
        ]
        hk = [nu[k + 1] + SHIFT * nu[k] for k in range(5)]
        l10 = hk[1] / hk[0]
        l20 = hk[2] / hk[0]
        d1 = hk[2] - l10 * hk[1]
        s21 = hk[3] - l20 * hk[1]
        l21 = s21 / d1
        d2 = hk[4] - l20 * hk[2] - l21 * s21
        y1 = nu[1] - l10 * nu[0]
        y2 = nu[2] - l20 * nu[0] - l21 * y1
        c2 = y2 / d2
        c1 = y1 / d1 - l21 * c2
        c0 = nu[0] / hk[0] - l10 * c1 - l20 * c2

        def combine(i, carry):
            here = pl.ds(pl.multiple_of(i * RB + PAD, PAD), RB)
            vec[0, c, here, :] = (
                c0 * vec[0, c, here, :] + c1 * vec[1, c, here, :] + c2 * vec[2, c, here, :]
            )
            return carry

        lax.fori_loop(0, lrows // RB, combine, 0)
        store = pltpu.make_async_copy(
            vec.at[0, c, pl.ds(PAD, lrows), :], lake_out.at[c], loc.at[c]
        )
        store.start()
        stores.append(store)

    def sent_sums(k, carry):
        sum_copy(peer(k), me).wait_send()
        return carry

    lax.fori_loop(1, n, sent_sums, 0)
    slope_store.wait()
    height_store.wait()
    for store in stores:
        store.wait()


def per_device(
    n0,
    n1,
    slope_depth,
    slope_momentum,
    bed_slope,
    friction,
    slope_active,
    owners,
    offsets,
    lake_height,
    lake_momentum,
    lake_diagonal,
):
    n = n0 * n1
    rows, cols = slope_depth.shape
    lrows = lake_height.shape[0]
    cap = -(-max(2, 2 * rows // n) // 8) * 8
    slots = n * cap
    f32 = jnp.float32
    dma = pltpu.SemaphoreType.DMA
    vmem = pl.BlockSpec(memory_space=pltpu.VMEM)
    hbm = pl.BlockSpec(memory_space=pl.ANY)
    return pl.pallas_call(
        functools.partial(kernel, n0, n1, cap),
        out_shape=(
            jax.ShapeDtypeStruct((3, rows, cols), f32),
            jax.ShapeDtypeStruct((lrows, cols), f32),
            jax.ShapeDtypeStruct((2, lrows, cols), f32),
        ),
        in_specs=[vmem] * 8 + [hbm] * 3,
        out_specs=(hbm,) * 3,
        scratch_shapes=[
            pltpu.VMEM((SECTIONS + 1, 3, rows + 2 * PAD, cols), f32),
            pltpu.VMEM((3, rows, 3 * cols), jnp.bfloat16),
            pltpu.VMEM((slots, 3 * cols), f32),
            pltpu.VMEM((slots, 3 * cols), f32),
            pltpu.VMEM((slots, 128), f32),
            pltpu.VMEM((slots, 128), f32),
            pltpu.VMEM((lrows, slots), jnp.bfloat16),
            pltpu.VMEM((3, slots, cols), jnp.bfloat16),
            pltpu.VMEM((3, 2, lrows + 2 * PAD, cols), f32),
            pltpu.VMEM((lrows, cols), f32),
            pltpu.VMEM((lrows, cols), f32),
            pltpu.VMEM((SECTIONS, 2, 3, cols), f32),
            pltpu.VMEM((SECTIONS, 2, 3, cols), f32),
            pltpu.VMEM((SECTIONS, 2, 3, rows), f32),
            pltpu.VMEM((SECTIONS, 2, 3, rows), f32),
            pltpu.VMEM((3, 2, 2, cols), f32),
            pltpu.VMEM((3, 2, 2, cols), f32),
            pltpu.VMEM((3, 2, 2, lrows), f32),
            pltpu.VMEM((3, 2, 2, lrows), f32),
            pltpu.VMEM((1, 128), f32),
            pltpu.VMEM((n, 1, 128), f32),
            dma((n,)),
            dma((n,)),
            dma((n,)),
            dma((n,)),
            dma((SECTIONS, 4)),
            dma((SECTIONS, 4)),
            dma((3, 4)),
            dma((3, 4)),
            dma((n,)),
            dma((n,)),
            dma((7,)),
        ],
        compiler_params=pltpu.CompilerParams(
            collective_id=0, has_side_effects=True, vmem_limit_bytes=58 * 1024 * 1024
        ),
    )(
        slope_depth,
        slope_momentum,
        bed_slope,
        friction,
        slope_active,
        owners.reshape(1, rows),
        owners.reshape(rows, 1),
        offsets.reshape(1, rows),
        lake_height,
        lake_momentum,
        lake_diagonal,
    )


def solution(mesh):
    return jax.shard_map(
        functools.partial(per_device, mesh.shape["gx"], mesh.shape["gy"]),
        mesh=mesh,
        in_specs=(
            P("gx", "gy"),
            P(None, "gx", "gy"),
            P(None, "gx", "gy"),
            P("gx", "gy"),
            P("gx", "gy"),
            P("gx", "gy", None, None),
            P("gx", "gy", None),
            P("gx", "gy"),
            P(None, "gx", "gy"),
            P("gx", "gy"),
        ),
        out_specs=(P(None, "gx", "gy"), P("gx", "gy"), P(None, "gx", "gy")),
        check_vma=False,
    )
```

time: 531 us -> 122 us (0.23); the launches traced: 524 us -> 122 us
  other arithmetic: 155 us -> 0 us
  blocking collectives: 126 us -> 0 us
  Pallas kernels: 0 us -> 114 us
  waiting for transfers between devices: 114 us -> 0 us
  starting transfers between devices: 59.8 us -> 0 us
  local copies, waits for them, and re-layouts: 66.3 us -> 6.6 us
    psum x3 -> x0, blocking collectives: 126 us -> none  [paired_sums(): lax.psum((jnp.sum(residual * residual, axis=(1, 2)), jnp.sum(residual * a...]
    pallas_call x0 -> x1, Pallas kernels: none -> 114 us  [per_device(): pl.pallas_call(functools.partial(kernel, n0, n1, cap), out_shape=(jax.Sha...]
    all_to_all x2 -> x0, waiting for transfers between devices: 72.5 us -> none  [the longest x1 72.5 us: per_device(): lax.all_to_all(payload, ('gx', 'gy'), split_axis=0, concat_axis=0, tiled=...]
    scatter-add x1 -> x0, other arithmetic: 66.9 us -> none  [per_device(): jnp.zeros((lake_rows + 1, 3, columns), jnp.float32).at[landing]]
    reduce_sum x4 -> x0, other arithmetic: 50.7 us -> none  [the longest x3 50.6 us: paired_sums(): jnp.sum(residual * applied, axis=(1, 2))]
    ppermute x20 -> x0, starting transfers between devices: 43.8 us -> none  [the longest x10 30.1 us: with_halo(): before = lax.ppermute(last, axis, up)]
    ppermute x20 -> x0, waiting for transfers between devices: 42 us -> none  [the longest x10 31.1 us: with_halo(): before = lax.ppermute(last, axis, up)]
    scatter x2 -> x0, local copies, waits for them, and re-layouts: 27.9 us -> none  [the longest x1 26.5 us: per_device(): jnp.zeros((devices * capacity, 3, columns), jnp.float32).at[slot_index]]
  transfers between devices with their start and end apart: 22 -> 0, of which waited for: 10 -> 0; matrix products, arithmetic and copies ran while one was open for 11% -> 0% of each run, Pallas kernels for 0% -> 0%
where the time goes in v1:
time: 122 us
  Pallas kernels  114 us (93%)
  local copies, waits for them, and re-layouts  6.6 us (5%)
    pallas_call x1, Pallas kernels, per_device(): pl.pallas_call(functools.partial(kernel, n0, n1, cap), out_shape=(jax.Sha...  114 us
    unnamed x7, local copies, waits for them, and re-layouts  5.12 us

profile of v1, /device:TPU:0, one launch (start us, length us, event | category | flops | bytes accessed | tf_op | source)
XLA Modules:
  0.0 121.6 jit_solution(2828138314154514009)
XLA Ops:
  0.6 1.5 %copy.13.own_col_ref = s32[256,1]{1,0:T(8,128)} copy(s32[256,1]{0,1:T(1,128)} %bitcast.3) | data formatting | bytes 2048 | tf_op jit(solution)/shard_map/reshape | solution.py:602
  2.1 114.4 %shard_map.121 = (f32[3,256,512]{2,1,0:T(8,128)}, f32[512,512]{1,0:T(8,128)}, f32[2,512,512]{2,1,0:T(8,128)}) custom-call(f32[256,512]{1,0:T(8,128)} %depth_ref.1, f32[2,256,512]{2,1,0:T(8,128)} %mom_ref.1, f32[2,256,512]{2,1,0:T(8,128)} %bed_ref.1, f32[256,512]{1,0:T(8,128)} %fric_ref.1, s32[256,512]{1,0:T(8,128)} %act_ref.1, s32[1,256]{1,0:T(1,128)} %bitcast.4, ...), custom_call_target="tpu_custom_call" | custom-call | tf_op jit(solution)/shard_map/pallas_call | solution.py:549
  116.5 0.0 copy-start.1
  116.5 0.0 copy-start
  116.5 2.8 %copy.17 = f32[3,256,512]{2,1,0:T(8,128)} copy(f32[3,256,512]{2,1,0:T(8,128)} %get-tuple-element.6) | data formatting | bytes 3145728
  119.3 0.0 copy-done.1
  119.3 1.0 copy.18
  120.3 0.0 copy-done
  120.3 1.3 %copy.19 = f32[2,512,512]{2,1,0:T(8,128)} copy(f32[2,512,512]{2,1,0:T(8,128)S(1)} %copy-done) | data formatting | bytes 4194304
Async XLA Ops:
  116.5 2.8 %copy-start.1 = (f32[512,512]{1,0:T(8,128)S(1)}, f32[512,512]{1,0:T(8,128)}, u32[]{:S(2)}) copy-start(f32[512,512]{1,0:T(8,128)} %get-tuple-element.7) | copy-start | bytes 3145732
  116.5 3.8 %copy-start = (f32[2,512,512]{2,1,0:T(8,128)S(1)}, f32[2,512,512]{2,1,0:T(8,128)}, u32[]{:S(2)}) copy-start(f32[2,512,512]{2,1,0:T(8,128)} %get-tuple-element.8) | copy-start | bytes 6291460

commit v2 on v1

--- a/solution.py
+++ b/solution.py
@@ -50,13 +50,12 @@
     n0,
     n1,
     cap,
-    depth_ref,
-    mom_ref,
-    bed_ref,
-    fric_ref,
-    act_ref,
+    depth_hbm,
+    mom_hbm,
+    bed_hbm,
+    fric_hbm,
+    act_hbm,
     own_row_ref,
-    own_col_ref,
     off_ref,
     lh_hbm,
     lm_hbm,
@@ -72,6 +71,9 @@
     tag_recv,
     hot,
     rparts,
+    bed_ref,
+    fric_ref,
+    act_ref,
     vec,
     lh,
     ld,
@@ -101,7 +103,7 @@
     gx = lax.axis_index("gx")
     gy = lax.axis_index("gy")
     me = gx * n1 + gy
-    rows, cols = depth_ref.shape
+    rows, cols = fric_ref.shape
     lrows = lh.shape[0]
     slots = n * cap
     f32 = jnp.float32
@@ -112,14 +114,23 @@
     def coords(t):
         return (lax.div(t, n1), lax.rem(t, n1))
 
+    load_f = [
+        pltpu.make_async_copy(src, fields.at[0, c, pl.ds(PAD, rows), :], loc.at[7 + c])
+        for c, src in enumerate((depth_hbm, mom_hbm.at[0], mom_hbm.at[1]))
+    ]
+    load_s = [
+        pltpu.make_async_copy(bed_hbm, bed_ref, loc.at[10]),
+        pltpu.make_async_copy(fric_hbm, fric_ref, loc.at[11]),
+        pltpu.make_async_copy(act_hbm, act_ref, loc.at[12]),
+    ]
+    for c in load_f + load_s:
+        c.start()
     load_m = [
         pltpu.make_async_copy(lm_hbm.at[c], vec.at[0, c, pl.ds(PAD, lrows), :], loc.at[c])
         for c in range(2)
     ]
     load_h = pltpu.make_async_copy(lh_hbm, lh, loc.at[2])
     load_d = pltpu.make_async_copy(ld_hbm, ld, loc.at[3])
-    for c in load_m + [load_h, load_d]:
-        c.start()
 
     barrier = pltpu.get_barrier_semaphore()
 
@@ -130,13 +141,15 @@
     lax.fori_loop(1, n, greet, 0)
 
     own_row = own_row_ref[...]
+    own_real = own_row.astype(f32)
+    own_col = as_column(own_real)[:, 0:1]
     before = lax.broadcasted_iota(jnp.int32, (rows, rows), 0) < lax.broadcasted_iota(
         jnp.int32, (rows, rows), 1
     )
     rank = jnp.sum(
-        jnp.where((own_col_ref[...] == own_row) & before, 1.0, 0.0), axis=0, keepdims=True
+        jnp.where((own_col == own_real) & before, 1.0, 0.0), axis=0, keepdims=True
     )
-    slot = own_row * cap + rank.astype(jnp.int32)
+    slot = lax.rem(own_row - me + n, n) * cap + rank.astype(jnp.int32)
     off = (off_ref[...] + 1).astype(f32)
     SC = 128
 
@@ -158,32 +171,31 @@
         for e in range(3):
             vec[e, c, 0:PAD, :] = jnp.zeros((PAD, cols), f32)
             vec[e, c, PAD + lrows : PAD + lrows + PAD, :] = jnp.zeros((PAD, cols), f32)
-    fields[0, 0, PAD : PAD + rows, :] = depth_ref[...]
-    fields[0, 1, PAD : PAD + rows, :] = mom_ref[0]
-    fields[0, 2, PAD : PAD + rows, :] = mom_ref[1]
-
-    pl.semaphore_wait(barrier, n - 1)
-
-    def at(t):
-        return pl.ds(pl.multiple_of(t * cap, cap), cap)
-
-    def tag_copy(t, s):
+    for c in load_m + [load_h, load_d]:
+        c.start()
+    for c in load_f:
+        c.wait()
+
+    def at(k):
+        return pl.ds(pl.multiple_of(k * cap, cap), cap)
+
+    def tag_copy(k):
         return pltpu.make_async_remote_copy(
-            src_ref=tag_send.at[at(t), :],
-            dst_ref=tag_recv.at[at(s), :],
-            send_sem=tag_ss.at[t],
-            recv_sem=tag_rs.at[s],
-            device_id=coords(t),
+            src_ref=tag_send.at[at(k), :],
+            dst_ref=tag_recv.at[at(k), :],
+            send_sem=tag_ss.at[k],
+            recv_sem=tag_rs.at[k],
+            device_id=coords(peer(k)),
             device_id_type=MESH,
         )
 
-    def blk_copy(t, s):
+    def blk_copy(k):
         return pltpu.make_async_remote_copy(
-            src_ref=send.at[at(t), :],
-            dst_ref=recv.at[at(s), :],
-            send_sem=blk_ss.at[t],
-            recv_sem=blk_rs.at[s],
-            device_id=coords(t),
+            src_ref=send.at[at(k), :],
+            dst_ref=recv.at[at(k), :],
+            send_sem=blk_ss.at[k],
+            recv_sem=blk_rs.at[k],
+            device_id=coords(peer(k)),
             device_id_type=MESH,
         )
 
@@ -237,16 +249,20 @@
         for c, x in enumerate(across_terms(*left, -1.0)):
             scol_s[e, 1, c : c + 1, :] = column(x, 0)
         copies = halo_copies(e, srow_s, srow_r, scol_s, scol_r, sl_ss, sl_rs)
+        if e == 0:
+            pl.semaphore_wait(barrier, n - 1)
         for c in copies:
             c.start()
         pending += copies
         if e == 0:
 
             def send_tags(k, carry):
-                tag_copy(peer(k), me).start()
+                tag_copy(k).start()
                 return carry
 
             lax.fori_loop(1, n, send_tags, 0)
+            for c in load_s:
+                c.wait()
 
         def section(i, carry):
             base = pl.multiple_of(i * RB, RB)
@@ -298,6 +314,12 @@
         for p in range(3):
             parts[p, :, c * cols : (c + 1) * cols] = pieces[p]
 
+    per = SC // cap
+
+    def send_block(k, carry):
+        blk_copy(k).start()
+        return carry
+
     def pack(j, carry):
         pick = jnp.where(chosen(j), 1.0, 0.0).astype(jnp.bfloat16)
         dst = pl.ds(pl.multiple_of(j * SC, SC), SC)
@@ -307,22 +329,18 @@
             total += jnp.dot(pick, parts[1, :, w], preferred_element_type=f32)
             total += jnp.dot(pick, parts[0, :, w], preferred_element_type=f32)
             send[dst, w] = total
+        lax.fori_loop(lax.max(j * per, 1), (j + 1) * per, send_block, 0)
         return carry
 
     lax.fori_loop(0, slots // SC, pack, 0)
 
-    def send_blocks(k, carry):
-        blk_copy(peer(k), me).start()
-        return carry
-
-    lax.fori_loop(1, n, send_blocks, 0)
-    own_tags = pltpu.make_async_copy(tag_send.at[at(me), :], tag_recv.at[at(me), :], loc.at[5])
-    own_blk = pltpu.make_async_copy(send.at[at(me), :], recv.at[at(me), :], loc.at[6])
+    own_tags = pltpu.make_async_copy(tag_send.at[at(0), :], tag_recv.at[at(0), :], loc.at[5])
+    own_blk = pltpu.make_async_copy(send.at[at(0), :], recv.at[at(0), :], loc.at[6])
     own_tags.start()
     own_blk.start()
 
     def got_tags(k, carry):
-        tag_copy(peer(k), peer(k)).wait_recv()
+        tag_copy(k).wait_recv()
         return carry
 
     lax.fori_loop(1, n, got_tags, 0)
@@ -331,48 +349,49 @@
 
     def land(i, carry):
         want = (lax.broadcasted_iota(jnp.int32, (SC, slots), 0) + (i * SC + 1)).astype(f32)
-        hot[pl.ds(pl.multiple_of(i * SC, SC), SC), :] = jnp.where(want == tag_row, 1.0, 0.0).astype(
-            jnp.bfloat16
-        )
+        pick = jnp.where(want == tag_row, 1.0, 0.0).astype(jnp.bfloat16)
+        for q in range(slots // SC):
+            hot[q, pl.ds(pl.multiple_of(i * SC, SC), SC), :] = pick[:, q * SC : (q + 1) * SC]
         return carry
 
     lax.fori_loop(0, lrows // SC, land, 0)
     for c in load_m + [load_h, load_d]:
         c.wait()
 
-    def got_blocks(k, carry):
-        blk_copy(peer(k), peer(k)).wait_recv()
-        return carry
-
-    lax.fori_loop(1, n, got_blocks, 0)
     own_blk.wait()
 
-    for c in range(3):
-
-        def cut(j, carry):
-            here = pl.ds(pl.multiple_of(j * SC, SC), SC)
-            for p, piece in enumerate(split3(recv[here, c * cols : (c + 1) * cols])):
-                rparts[p, here, :] = piece
-            return carry
-
-        lax.fori_loop(0, slots // SC, cut, 0)
-
-        def inflow(i, carry):
+    def got_block(k, carry):
+        blk_copy(k).wait_recv()
+        return carry
+
+    def arrive(q, carry):
+        lax.fori_loop(lax.max(q * per, 1), (q + 1) * per, got_block, 0)
+        for c in range(3):
+            w = slice(c * cols, (c + 1) * cols)
+            pieces = split3(recv[pl.ds(pl.multiple_of(q * SC, SC), SC), w])
+            for p in range(3):
+                rparts[p, :, w] = pieces[p]
+
+        def inflow(i, inner):
             here = pl.ds(pl.multiple_of(i * SC, SC), SC)
-            pick = hot[here, :]
-            total = jnp.dot(pick, rparts[2], preferred_element_type=f32)
-            total += jnp.dot(pick, rparts[1], preferred_element_type=f32)
-            total += jnp.dot(pick, rparts[0], preferred_element_type=f32)
-            if c == 0:
-                lh[here, :] += total
-            else:
-                vec[0, c - 1, pl.ds(pl.multiple_of(i * SC + PAD, PAD), SC), :] += total
-            return carry
+            pick = hot[q, here, :]
+            for c in range(3):
+                w = slice(c * cols, (c + 1) * cols)
+                total = jnp.dot(pick, rparts[2, :, w], preferred_element_type=f32)
+                total += jnp.dot(pick, rparts[1, :, w], preferred_element_type=f32)
+                total += jnp.dot(pick, rparts[0, :, w], preferred_element_type=f32)
+                if c == 0:
+                    lh[here, :] += total
+                else:
+                    vec[0, c - 1, pl.ds(pl.multiple_of(i * SC + PAD, PAD), SC), :] += total
+            return inner
 
         lax.fori_loop(0, lrows // SC, inflow, 0)
-        if c == 0:
-            height_store = pltpu.make_async_copy(lh, height_out, loc.at[2])
-            height_store.start()
+        return carry
+
+    lax.fori_loop(0, slots // SC, arrive, 0)
+    height_store = pltpu.make_async_copy(lh, height_out, loc.at[2])
+    height_store.start()
 
     spot = lax.broadcasted_iota(jnp.int32, (1, 128), 1)
     mine = jnp.zeros((1, 128), f32)
@@ -464,8 +483,8 @@
         c.wait_send()
 
     def sent(k, carry):
-        tag_copy(peer(k), me).wait_send()
-        blk_copy(peer(k), me).wait_send()
+        tag_copy(k).wait_send()
+        blk_copy(k).wait_send()
         return carry
 
     lax.fori_loop(1, n, sent, 0)
@@ -553,7 +572,7 @@
             jax.ShapeDtypeStruct((lrows, cols), f32),
             jax.ShapeDtypeStruct((2, lrows, cols), f32),
         ),
-        in_specs=[vmem] * 8 + [hbm] * 3,
+        in_specs=[hbm] * 5 + [vmem] * 2 + [hbm] * 3,
         out_specs=(hbm,) * 3,
         scratch_shapes=[
             pltpu.VMEM((SECTIONS + 1, 3, rows + 2 * PAD, cols), f32),
@@ -562,8 +581,11 @@
             pltpu.VMEM((slots, 3 * cols), f32),
             pltpu.VMEM((slots, 128), f32),
             pltpu.VMEM((slots, 128), f32),
-            pltpu.VMEM((lrows, slots), jnp.bfloat16),
-            pltpu.VMEM((3, slots, cols), jnp.bfloat16),
+            pltpu.VMEM((slots // 128, lrows, 128), jnp.bfloat16),
+            pltpu.VMEM((3, 128, 3 * cols), jnp.bfloat16),
+            pltpu.VMEM((2, rows, cols), f32),
+            pltpu.VMEM((rows, cols), f32),
+            pltpu.VMEM((rows, cols), slope_active.dtype),
             pltpu.VMEM((3, 2, lrows + 2 * PAD, cols), f32),
             pltpu.VMEM((lrows, cols), f32),
             pltpu.VMEM((lrows, cols), f32),
@@ -587,7 +609,7 @@
             dma((3, 4)),
             dma((n,)),
             dma((n,)),
-            dma((7,)),
+            dma((13,)),
         ],
         compiler_params=pltpu.CompilerParams(
             collective_id=0, has_side_effects=True, vmem_limit_bytes=58 * 1024 * 1024
@@ -599,7 +621,6 @@
         friction,
         slope_active,
         owners.reshape(1, rows),
-        owners.reshape(rows, 1),
         offsets.reshape(1, rows),
         lake_height,
         lake_momentum,

time: 122 us -> 114 us (0.934)
  Pallas kernels: 114 us -> 108 us
  local copies, waits for them, and re-layouts: 6.6 us -> 5.12 us
    pallas_call x1, Pallas kernels: 114 us -> 108 us  [per_device(): pl.pallas_call(functools.partial(kernel, n0, n1, cap), out_shape=(jax.Sha...]
    reshape x1 -> x0, local copies, waits for them, and re-layouts: 1.47 us -> none  [per_device(): owners.reshape(rows, 1)]
where the time goes in v2:
time: 114 us
  Pallas kernels  108 us (95%)
  local copies, waits for them, and re-layouts  5.12 us (4%)
    pallas_call x1, Pallas kernels, per_device(): pl.pallas_call(functools.partial(kernel, n0, n1, cap), out_shape=(jax.Sha...  108 us
    unnamed x7, local copies, waits for them, and re-layouts  5.12 us

profile of v2, /device:TPU:0, one launch (start us, length us, event | category | flops | bytes accessed | tf_op | source)
XLA Modules:
  0.0 113.7 jit_solution(2439036423899030222)
XLA Ops:
  0.6 107.9 %shard_map.121 = (f32[3,256,512]{2,1,0:T(8,128)}, f32[512,512]{1,0:T(8,128)}, f32[2,512,512]{2,1,0:T(8,128)}) custom-call(f32[256,512]{1,0:T(8,128)} %depth_hbm.1, f32[2,256,512]{2,1,0:T(8,128)} %mom_hbm.1, f32[2,256,512]{2,1,0:T(8,128)} %bed_hbm.1, f32[256,512]{1,0:T(8,128)} %fric_hbm.1, s32[256,512]{1,0:T(8,128)} %act_hbm.1, s32[1,256]{1,0:T(1,128)} %bitcast.2, ...), custom_call_target="tpu_custom_call" | custom-call | tf_op jit(solution)/shard_map/pallas_call | solution.py:568
  108.6 0.0 copy-start.1
  108.6 0.0 copy-start
  108.6 2.8 %copy.16 = f32[3,256,512]{2,1,0:T(8,128)} copy(f32[3,256,512]{2,1,0:T(8,128)} %get-tuple-element.6) | data formatting | bytes 3145728
  111.4 0.0 copy-done.1
  111.4 1.0 copy.17
  112.4 0.0 copy-done
  112.4 1.3 %copy.18 = f32[2,512,512]{2,1,0:T(8,128)} copy(f32[2,512,512]{2,1,0:T(8,128)S(1)} %copy-done) | data formatting | bytes 4194304
Async XLA Ops:
  108.6 2.8 %copy-start.1 = (f32[512,512]{1,0:T(8,128)S(1)}, f32[512,512]{1,0:T(8,128)}, u32[]{:S(2)}) copy-start(f32[512,512]{1,0:T(8,128)} %get-tuple-element.7) | copy-start | bytes 3145732
  108.6 3.8 %copy-start = (f32[2,512,512]{2,1,0:T(8,128)S(1)}, f32[2,512,512]{2,1,0:T(8,128)}, u32[]{:S(2)}) copy-start(f32[2,512,512]{2,1,0:T(8,128)} %get-tuple-element.8) | copy-start | bytes 6291460

commit v3 on v2

--- a/solution.py
+++ b/solution.py
@@ -224,7 +224,7 @@
         return out
 
     pending = []
-    RB = 64
+    RB = 16
     lane = lax.broadcasted_iota(jnp.int32, (RB, cols), 1)
     first_lane = lane == 0
     last_lane = lane == cols - 1

time: 114 us -> 120 us (1.053)
  Pallas kernels: 108 us -> 114 us
    pallas_call x1, Pallas kernels: 108 us -> 114 us  [per_device(): pl.pallas_call(functools.partial(kernel, n0, n1, cap), out_shape=(jax.Sha...]
where the time goes in v3:
time: 120 us
  Pallas kernels  114 us (95%)
  local copies, waits for them, and re-layouts  5.12 us (4%)
    pallas_call x1, Pallas kernels, per_device(): pl.pallas_call(functools.partial(kernel, n0, n1, cap), out_shape=(jax.Sha...  114 us
    unnamed x7, local copies, waits for them, and re-layouts  5.12 us

profile of v3, /device:TPU:0, one launch (start us, length us, event | category | flops | bytes accessed | tf_op | source)
XLA Modules:
  0.0 120.1 jit_solution(6147159158942800231)
XLA Ops:
  0.6 114.3 %shard_map.121 = (f32[3,256,512]{2,1,0:T(8,128)}, f32[512,512]{1,0:T(8,128)}, f32[2,512,512]{2,1,0:T(8,128)}) custom-call(f32[256,512]{1,0:T(8,128)} %depth_hbm.1, f32[2,256,512]{2,1,0:T(8,128)} %mom_hbm.1, f32[2,256,512]{2,1,0:T(8,128)} %bed_hbm.1, f32[256,512]{1,0:T(8,128)} %fric_hbm.1, s32[256,512]{1,0:T(8,128)} %act_hbm.1, s32[1,256]{1,0:T(1,128)} %bitcast.2, ...), custom_call_target="tpu_custom_call" | custom-call | tf_op jit(solution)/shard_map/pallas_call | solution.py:568
  114.9 0.0 copy-start.1
  115.0 0.0 copy-start
  115.0 2.8 %copy.16 = f32[3,256,512]{2,1,0:T(8,128)} copy(f32[3,256,512]{2,1,0:T(8,128)} %get-tuple-element.6) | data formatting | bytes 3145728
  117.8 0.0 copy-done.1
  117.8 1.0 copy.17
  118.8 0.0 copy-done
  118.8 1.3 %copy.18 = f32[2,512,512]{2,1,0:T(8,128)} copy(f32[2,512,512]{2,1,0:T(8,128)S(1)} %copy-done) | data formatting | bytes 4194304
Async XLA Ops:
  114.9 2.8 %copy-start.1 = (f32[512,512]{1,0:T(8,128)S(1)}, f32[512,512]{1,0:T(8,128)}, u32[]{:S(2)}) copy-start(f32[512,512]{1,0:T(8,128)} %get-tuple-element.7) | copy-start | bytes 3145732
  115.0 3.8 %copy-start = (f32[2,512,512]{2,1,0:T(8,128)S(1)}, f32[2,512,512]{2,1,0:T(8,128)}, u32[]{:S(2)}) copy-start(f32[2,512,512]{2,1,0:T(8,128)} %get-tuple-element.8) | copy-start | bytes 6291460
